TPU v7x, 512 devices: a whole 4x4x16 slice. The times are simulated.
512 devices in a mesh: prompt: 32 (over z, core), sample: 4 (over y), tensor: 4 (over x).
Axes of the slice: x: 4, y: 4, z: 16, core: 2. Of those that a mesh axis runs over, the one named last changes fastest.
Arguments:
- queries: bfloat16 [3, 160, 64, 128], P(None, 'sample', 'tensor'), may hold values from -12 to 65, as said below
- prefix_keys: bfloat16 [10, 16384, 8, 128], P(None, ('prompt', 'sample'), 'tensor'), may hold values from -9 to 40, as said below
- prefix_values: bfloat16 [10, 16384, 8, 128], P(None, ('prompt', 'sample'), 'tensor'), may hold values from -192 to 192
- suffix_keys: bfloat16 [160, 8, 8, 128], P('sample', None, 'tensor'), may hold values from -20 to 20
- suffix_values: bfloat16 [160, 8, 8, 128], P('sample', None, 'tensor'), may hold values from -192 to 192
- new_keys: bfloat16 [3, 160, 8, 128], P(None, 'sample', 'tensor'), may hold values from -20 to 20
- new_values: bfloat16 [3, 160, 8, 128], P(None, 'sample', 'tensor'), may hold values from -192 to 192
- prompt_lengths: int32 [10], replicated, may hold values from 5461 to 16384, as said below
- unfinished: int32 [3, 10], replicated, may hold values from 1 to 16, as said below
- slot_sample: int32 [160], replicated, may hold values from 0 to 159, each once
Outputs:
- attended: bfloat16 [3, 160, 64, 128], P(None, 'sample', 'tensor')
Inputs may be any that keep to these rules, and one draw needn't show every extreme that they name: `queries`: query vectors of the new tokens. `prefix_keys`: key vectors of the prompts' prefixes. `prompt_lengths`: prefix positions at or beyond a prompt's length are not keys. Some prompt has exactly 16384 positions and some exactly 5461. The samples of prompt p with index below unfinished[t, p] are still generating at step t. `slot_sample`: each sample of each prompt is held by exactly one slot.
All inputs are finite; a program needn't handle non-finite values.
Results may differ from a plain program's by a relative error of at most 0.003.
Values may be sent and summed in bfloat16 or wider, within the bound.
No kernel may reach another device: no remote copies, remote signals or barrier semaphores. Data moves between devices by JAX's collectives and lax.ppermute only.
A program may use at most 64 MiB of HBM per device.

v0:
```python
import math

import jax
import jax.numpy as jnp
from jax import lax
from jax.sharding import PartitionSpec as P

SAMPLES = 16


MASKED = -1e30


def slot_layout(values, slot_sample):
    moved = jnp.moveaxis(values, 2, 0)
    moved = jnp.swapaxes(moved, 2, 3)
    step_count, prompt_count, per_prompt, key_heads, group_size = moved.shape[:5]
    trailing = moved.shape[5:]
    merged = moved.reshape(
        (step_count, prompt_count * per_prompt, key_heads * group_size) + trailing
    )
    return jnp.take(merged, slot_sample, axis=1)


def shards(
    queries,
    prefix_keys,
    prefix_values,
    suffix_keys,
    suffix_values,
    new_keys,
    new_values,
    prompt_lengths,
    unfinished,
    slot_sample,
):
    step_count, local_slots, head_count, head_width = queries.shape
    prompt_count, span_rows, key_heads, _ = prefix_keys.shape
    group_size = head_count // key_heads
    per_prompt = SAMPLES
    score_scale = 1.0 / math.sqrt(head_width)
    sample_slot = jnp.argsort(slot_sample)
    device_rank = lax.axis_index("prompt") * lax.axis_size("sample") + lax.axis_index("sample")
    positions = device_rank * span_rows + jnp.arange(span_rows, dtype=jnp.int32)
    own_first = lax.axis_index("sample") * local_slots
    every_query = lax.all_gather(queries, "sample", axis=1, tiled=True)
    sorted_query = jnp.take(every_query, sample_slot, axis=1)
    sorted_query = sorted_query.reshape(
        step_count, prompt_count, per_prompt, key_heads, group_size, head_width
    )
    sorted_query = jnp.transpose(sorted_query, (1, 3, 0, 2, 4, 5))

    def prefix_scores(inputs):
        query_block, key_block, length = inputs
        scores = (
            jnp.einsum(
                "jtsgd,ljd->jtsgl", query_block, key_block, preferred_element_type=jnp.float32
            )
            * score_scale
        )
        scores = jnp.where(positions < length, scores, MASKED)
        return (scores, jnp.max(scores, axis=-1))

    scores, prefix_top = lax.map(prefix_scores, (sorted_query, prefix_keys, prompt_lengths))
    slot_top = slot_layout(prefix_top, slot_sample)
    own_query = queries.reshape(step_count, local_slots, key_heads, group_size, head_width)
    suffix_scores = (
        jnp.einsum("tajgd,aujd->tajgu", own_query, suffix_keys, preferred_element_type=jnp.float32)
        * score_scale
    )
    new_scores = (
        jnp.einsum("tajgd,uajd->tajgu", own_query, new_keys, preferred_element_type=jnp.float32)
        * score_scale
    )
    step_ids = jnp.arange(step_count, dtype=jnp.int32)
    causal = (step_ids[None, :] <= step_ids[:, None])[:, None, None, None, :]
    new_scores = jnp.where(causal, new_scores, MASKED)
    own_top = jnp.maximum(suffix_scores.max(-1), new_scores.max(-1)).reshape(
        step_count, local_slots, head_count
    )
    current = lax.dynamic_slice_in_dim(slot_top, own_first, local_slots, 1)
    row_top = lax.dynamic_update_slice_in_dim(slot_top, jnp.maximum(current, own_top), own_first, 1)
    row_top = lax.pmax(row_top, ("prompt", "sample"))
    sorted_top = jnp.take(row_top, sample_slot, axis=1)
    sorted_top = sorted_top.reshape(step_count, prompt_count, per_prompt, key_heads, group_size)
    sorted_top = jnp.transpose(sorted_top, (1, 3, 0, 2, 4))

    def prefix_sums(inputs):
        score_block, top_block, value_block, length = inputs
        weights = jnp.where(
            positions < length, jnp.exp(score_block - top_block[..., None]), 0.0
        ).astype(jnp.bfloat16)
        numerator = jnp.einsum(
            "jtsgl,ljd->jtsgd", weights, value_block, preferred_element_type=jnp.float32
        )
        return (numerator, jnp.sum(weights, axis=-1, dtype=jnp.float32))

    numerator, denominator = lax.map(
        prefix_sums, (scores, sorted_top, prefix_values, prompt_lengths)
    )
    numerator = slot_layout(numerator, slot_sample)
    denominator = slot_layout(denominator, slot_sample)
    own_row_top = lax.dynamic_slice_in_dim(row_top, own_first, local_slots, 1)
    own_row_top = own_row_top.reshape(step_count, local_slots, key_heads, group_size, 1)
    suffix_weights = jnp.exp(suffix_scores - own_row_top).astype(jnp.bfloat16)
    new_weights = jnp.where(causal, jnp.exp(new_scores - own_row_top), 0.0).astype(jnp.bfloat16)
    own_numerator = jnp.einsum(
        "tajgu,aujd->tajgd", suffix_weights, suffix_values, preferred_element_type=jnp.float32
    )
    own_numerator = own_numerator + jnp.einsum(
        "tajgu,uajd->tajgd", new_weights, new_values, preferred_element_type=jnp.float32
    )
    own_numerator = own_numerator.reshape(step_count, local_slots, head_count, head_width)
    own_denominator = jnp.sum(suffix_weights, axis=-1, dtype=jnp.float32) + jnp.sum(
        new_weights, axis=-1, dtype=jnp.float32
    )
    own_denominator = own_denominator.reshape(step_count, local_slots, head_count)
    own_ids = lax.dynamic_slice_in_dim(slot_sample, own_first, local_slots, 0)
    own_prompt = own_ids // per_prompt
    own_index = own_ids % per_prompt
    matches = own_prompt[:, None] == jnp.arange(prompt_count, dtype=jnp.int32)[None, :]
    still_going = jnp.sum(jnp.where(matches[None, :, :], unfinished[:, None, :], 0), axis=-1)
    living = (own_index[None, :] < still_going)[:, :, None, None]
    total_numerator, total_denominator = lax.psum((numerator, denominator), ("prompt", "sample"))
    total_numerator = lax.dynamic_slice_in_dim(total_numerator, own_first, local_slots, 1)
    total_denominator = lax.dynamic_slice_in_dim(total_denominator, own_first, local_slots, 1)
    combined = (total_numerator + own_numerator) / (total_denominator + own_denominator)[..., None]
    result = jnp.where(living, combined, 0.0).astype(jnp.bfloat16)
    return result


def solution(mesh):
    in_specs = (
        P(None, "sample", "tensor", None),
        P(None, ("prompt", "sample"), "tensor", None),
        P(None, ("prompt", "sample"), "tensor", None),
        P("sample", None, "tensor", None),
        P("sample", None, "tensor", None),
        P(None, "sample", "tensor", None),
        P(None, "sample", "tensor", None),
        P(),
        P(),
        P(),
    )
    out_specs = P(None, "sample", "tensor", None)
    return jax.shard_map(shards, mesh=mesh, in_specs=in_specs, out_specs=out_specs, check_vma=False)
```

profile of v0, /device:TPU:1, one launch (start us, length us, event | category | flops | bytes accessed | tf_op | source)
XLA Modules:
  0.0 1170.5 jit_solution(1669467759202870620)
XLA Ops:
  7.3 3.8 sort.17
  12.4 2.8 fusion.16
  15.9 2.8 fusion.26
  21.4 30.9 %all-gather.2.cloned.1.call-done = bf16[3,160,16,128]{3,2,1,0:T(8,128)(2,1)} async-done(((bf16[3,40,16,128]{3,2,1,0:T(8,128)(2,1)}), bf16[3,160,16,128]{3,2,1,0:T(8,128)(2,1)}) %all-gather.2.cloned.1.call-update) | async-done | bytes 1966096 | tf_op jit(solution)/shard_map/all_gather | solution.py:46
  52.3 2.6 gather_fusion
  55.6 40.2 %while.26 = (s32[]{:T(128)}, f32[10,2,3,16,8,128]{5,4,3,2,1,0:T(8,128)}, f32[10,2,3,16,8]{4,3,2,1,0:T(8,128)S(1)}, s32[10]{0:T(128)}, bf16[10,2,3,16,8,128]{5,4,...) while((s32[]{:T(128)}, ...), condition=%wide.region_4.5_spmd.clone, body=%wide.region_2.4_spmd.clone.sunk | while | flops 25460224 | bytes 1676029 | solution.py:64
  55.6 1.3 dynamic_slice.82
  59.6 1.3 dynamic_slice.82
  63.6 1.3 dynamic_slice.82
  67.6 1.3 dynamic_slice.82
  71.6 1.3 dynamic_slice.82
  75.6 1.3 dynamic_slice.82
  79.7 1.3 dynamic_slice.82
  83.7 1.3 dynamic_slice.82
  87.7 1.3 dynamic_slice.82
  91.7 1.3 dynamic_slice.82
  99.1 490.4 %pmax.7 = f32[3,160,16]{2,0,1:T(4,128)S(1)} all-reduce(f32[3,160,16]{2,0,1:T(4,128)S(1)} %maximum_dynamic-update-slice_fusion), channel_id=1, replica_groups=mesh['prompt'=32,'sample'=4,'tensor'=4] {'prompt','sample'}, use_global_device_ids=true, to_apply=%region_7.9 | all-reduce | flops 7680 | bytes 61440 | tf_op jit(solution)/shard_map/pmax | solution.py:83
  591.1 63.9 %while.27 = (s32[]{:T(128)}, f32[10,2,3,16,8,128]{5,4,1,3,0,2:T(8,128)}, f32[10,2,3,16,8]{4,3,2,1,0:T(8,128)S(1)}, s32[10]{0:T(128)}, f32[10,2,3,16,8,128]{5,4,3...) while((s32[]{:T(128)}, ...), condition=%wide.region_10.12_spmd.clone, body=%wide.region_8.11_spmd.clone.sunk | while | flops 25951744 | bytes 2284033 | solution.py:98
  591.1 1.3 dynamic_slice.87
  594.0 1.3 convolution_bitcast_fusion.2
  596.1 1.3 convert_reduce_fusion.4
  597.5 1.3 dynamic_slice.87
  600.4 1.3 convolution_bitcast_fusion.2
  602.5 1.3 convert_reduce_fusion.4
  603.8 1.3 dynamic_slice.87
  606.8 1.3 convolution_bitcast_fusion.2
  608.9 1.3 convert_reduce_fusion.4
  610.2 1.3 dynamic_slice.87
  613.2 1.3 convolution_bitcast_fusion.2
  615.3 1.3 convert_reduce_fusion.4
  616.6 1.3 dynamic_slice.87
  619.6 1.3 convolution_bitcast_fusion.2
  621.6 1.3 convert_reduce_fusion.4
  623.0 1.3 dynamic_slice.87
  628.0 1.3 convert_reduce_fusion.4
  629.4 1.3 dynamic_slice.87
  632.3 1.3 convolution_bitcast_fusion.2
  634.4 1.3 convert_reduce_fusion.4
  635.8 1.3 dynamic_slice.87
  640.8 1.3 convert_reduce_fusion.4
  642.2 1.3 dynamic_slice.87
  647.2 1.3 convert_reduce_fusion.4
  648.6 1.3 dynamic_slice.87
  653.6 1.3 convert_reduce_fusion.4
  655.0 4.8 gather_fusion.1
  659.8 4.4 select_bitcast_fusion
  668.6 491.5 %psum.15 = f32[3,160,16]{2,0,1:T(4,128)S(1)} all-reduce(f32[3,160,16]{2,0,1:T(4,128)S(1)} %select_bitcast_fusion.2), channel_id=1, replica_groups=mesh['prompt'=32,'sample'=4,'tensor'=4] {'prompt','sample'}, use_global_device_ids=true, to_apply=%region_12.14 | all-reduce | flops 7680 | bytes 61440 | tf_op jit(solution)/shard_map/psum | solution.py:124
  1161.2 1.7 fusion.14
  (203 shorter events, 73.3 us)
Async XLA Ops:
  6.5 1154.2 %copy-start = (bf16[40,8,2,128]{3,2,1,0:T(2,128)(2,1)S(1)}, bf16[40,8,2,128]{3,2,1,0:T(2,128)(2,1)}, u32[]{:S(2)}) copy-start(bf16[40,8,2,128]{3,2,1,0:T(2,128)(2,1)} %param.20) | copy-start | bytes 491524
  6.5 13.0 %copy-start.4 = (s32[160]{0:T(256)S(1)}, s32[160]{0:T(256)}, u32[]{:S(2)}) copy-start(s32[160]{0:T(256)} %param.25) | copy-start | bytes 1924
  6.5 45.7 %all-gather.2.cloned.1.call-start = ((), (), s32[]{:S(2)}) async-start(), calls=%async_computation | async-start | bytes 2457600 | tf_op jit(solution)/shard_map/all_gather | solution.py:46
  7.3 1153.9 %all-reduce.2.cloned.1.call-start = ((), (), s32[]{:S(2)}) async-start(), calls=%async_computation.1 | async-start | bytes 7864320 | tf_op jit(solution)/shard_map/psum | solution.py:124
  12.4 9.1 copy-start.8
  15.6 5.8 copy-start.1
  15.9 2.8 copy-start.10
  20.1 35.1 %copy-start.6 = (s32[1024]{0:T(1024)}, s32[1024]{0:T(1024)S(1)}, u32[]{:S(2)}) copy-start(s32[1024]{0:T(1024)S(1)} %pad_clamp_fusion.1) | copy-start | bytes 12292
  95.7 494.7 %copy-start.9 = (pred[160]{0:T(512)(128)(4,1)S(1)}, pred[160]{0:T(512)(128)(4,1)}, u32[]{:S(2)}) copy-start(pred[160]{0:T(512)(128)(4,1)} %copy-done.8) | copy-start | bytes 484
  591.1 63.9 %copy-start.5 = (s32[1024]{0:T(1024)S(1)}, s32[1024]{0:T(1024)}, u32[]{:S(2)}) copy-start(s32[1024]{0:T(1024)} %pad_clamp_fusion) | copy-start | bytes 12292
  654.9 4.8 copy-start.7
  664.1 0.7 copy-start.13
  664.1 0.7 copy-start.12
  664.1 0.9 copy-start.14
  664.1 1.3 copy-start.2
  664.1 1.5 copy-start.11
  664.8 495.4 %copy-start.3 = (bf16[3,40,2,128]{3,2,1,0:T(2,128)(2,1)S(1)}, bf16[3,40,2,128]{3,2,1,0:T(2,128)(2,1)}, u32[]{:S(2)}) copy-start(bf16[3,40,2,128]{3,2,1,0:T(2,128)(2,1)} %param.22) | copy-start | bytes 184324
Sparse Core Ops, SparseCore 0:
  9.5 42.7 all-gather.1
  664.3 357.0 all-reduce.1
where the time goes:
time: 1180 us; the launch traced here: 1170 us
  blocking collectives  982 us (83%)
  local copies, waits for them, and re-layouts  69.4 us (6%)
  other arithmetic  43.7 us (4%)
  waiting for transfers between devices  31.6 us (3%)
  matrix products  29.2 us (2%)
  between operations  13.8 us (1%)
    psum x1, blocking collectives, shards(): lax.psum((numerator, denominator), ('prompt', 'sample'))  492 us
    pmax x1, blocking collectives, shards(): row_top = lax.pmax(row_top, ('prompt', 'sample'))  490 us
    dynamic_slice x40, local copies, waits for them, and re-layouts, shards(): lax.map(prefix_scores, (sorted_query, prefix_keys, prompt_lengths))  43.9 us
    all_gather x1, waiting for transfers between devices, shards(): every_query = lax.all_gather(queries, 'sample', axis=1, tiled=True)  30.9 us
  transfers between devices with their start and end apart: 2, of which 1 were waited for; matrix products, arithmetic and copies ran while one was open for 2% of the time, Pallas kernels for 0%

commit v1 on v0

v1 whole, which is shorter than its diff:
```python
import math

import jax
import jax.numpy as jnp
import numpy as np
from jax import lax
from jax.experimental import pallas as pl
from jax.experimental.pallas import tpu as pltpu
from jax.sharding import PartitionSpec as P

SAMPLES = 16
MASKED = -1e30
ABSENT = -60000.0
F32 = jnp.float32
BF16 = jnp.bfloat16
TAKERS = [[(0, 0)], [(0, 1)], [(0, 2), (1, 0)], [(1, 1)], [(1, 2)],
          [(2, 0)], [(2, 1)], [(2, 2), (3, 0)], [(3, 1)], [(3, 2)]]
VMEM = pl.BlockSpec(memory_space=pltpu.VMEM)
SMEM = pl.BlockSpec(memory_space=pltpu.SMEM)
PARAMS = pltpu.CompilerParams(vmem_limit_bytes=40 * 1024 * 1024)


HBM = pl.BlockSpec(memory_space=pltpu.HBM)
HIGHEST = lax.Precision.HIGHEST


def send_kernel(core_ref, row_ref, slot_ref, slots_ref, k_hbm, v_hbm, q_hbm, out_hbm, mode_ref,
                k_ref, v_ref, q_ref, some_q, out_ref, list_ref, in_sem, out_sem):
    ins = []
    for n, (src, dst) in enumerate(((k_hbm, k_ref), (v_hbm, v_ref))):
        for i in range(2):
            part = pl.ds(i * 1280, 1280)
            ins.append(pltpu.make_async_copy(src.at[part], dst.at[part], in_sem.at[n * 2 + i]))
    ins.append(pltpu.make_async_copy(q_hbm, q_ref, in_sem.at[4]))
    for copy in ins:
        copy.start()
    outs = []
    for i in range(40):
        list_ref[i] = 0
    counts = [jnp.int32(0)] * 4
    for i in range(40):
        sample = slot_ref[row_ref[0] * 40 + i]
        to = (sample >= 40).astype(jnp.int32) + (sample >= 80).astype(jnp.int32) + (sample >= 120).astype(jnp.int32)
        n = jnp.where(to < 2, jnp.where(to == 0, counts[0], counts[1]), jnp.where(to == 2, counts[2], counts[3]))
        counts = [counts[k] + (to == k).astype(jnp.int32) for k in range(4)]
        mine = ((n & 1) == core_ref[0]) & (n < 20)
        list_ref[jnp.where(mine, to * 10 + (n >> 1), 40)] = i

    def quarter(a):
        return (a >= 40).astype(jnp.int32) + (a >= 80).astype(jnp.int32) + (a >= 120).astype(jnp.int32)

    pair = lax.broadcasted_iota(jnp.int32, (16, 160), 0)
    common = quarter(lax.broadcasted_iota(jnp.int32, (16, 160), 1)) * 4 + quarter(slots_ref[...])
    owed = jnp.sum(jnp.where(common == pair, 1.0, 0.0), axis=1, keepdims=True)
    mode_ref[0] = (jnp.max(owed) > 20.0).astype(jnp.int32)

    def leave(dst, at, size):
        rows = pl.ds(at, size)
        copy = pltpu.make_async_copy(out_ref.at[dst, rows], out_hbm.at[dst, rows], out_sem.at[len(outs)])
        copy.start()
        outs.append(copy)

    to = lax.broadcasted_iota(jnp.int32, (256, 256), 0)
    row = lax.broadcasted_iota(jnp.int32, (256, 256), 1)
    apart = jnp.where(row == (to % 128) * 2 + to // 128, 1.0, 0.0).astype(BF16)
    for n, ref in enumerate((k_ref, v_ref)):
        for i in range(2):
            ins[n * 2 + i].wait()
            for p in range(i * 5, i * 5 + 5):
                rows = jnp.dot(apart, ref[pl.ds(p * 256, 256), :], preferred_element_type=F32).astype(BF16)
                for h in range(2):
                    for y, b in TAKERS[p]:
                        out_ref[h * 4 + y, pl.ds(n * 384 + b * 128, 128), :] = rows[h * 128:h * 128 + 128]
            for dst in (2 * i, 2 * i + 1, 2 * i + 4, 2 * i + 5):
                leave(dst, n * 384, 384)
    ins[4].wait()
    for y in range(4):
        for i in range(10):
            slot = list_ref[y * 10 + i]
            for t in range(3):
                rows = q_ref[t, slot].astype(F32)
                for h in range(2):
                    some_q[h, y, t * 80 + i * 8:t * 80 + i * 8 + 8, :] = rows[h * 8:h * 8 + 8]
        for h in range(2):
            out_ref[h * 4 + y, pl.ds(768, 240), :] = some_q[h, y].astype(BF16)
            leave(h * 4 + y, 768, 240)
    for copy in outs:
        copy.wait()


def attend_kernel(mode_ref, block_ref, limit_ref, start_ref, met_ref, order_ref, heads_ref, extra_hbm,
                  o_ref, every_q, some_q, extra_ref, sem):
    @pl.when(mode_ref[0] == 0)
    def _():
        for src in range(8):
            every_q[pl.ds(src * 240, 240), :] = met_ref[src, pl.ds(768, 240), :].astype(F32)

    @pl.when(mode_ref[0] != 0)
    def _():
        copy = pltpu.make_async_copy(extra_hbm, extra_ref, sem)
        copy.start()
        copy.wait()
        every_q[...] = extra_ref[...].astype(F32)

    stride = jnp.where(mode_ref[0] == 0, 80, 160)
    order = order_ref[...]
    n = lax.broadcasted_iota(jnp.int32, (192, 128), 0)
    lane_of = (n // 96) * 64 + n % 12
    lanes = lax.broadcasted_iota(jnp.int32, (192, 128), 1)
    every_lse = jnp.zeros((8, 128), F32)
    for j in range(5):
        for r in range(8):
            start = start_ref[j * 8 + r]
            for t in range(3):
                row = pl.multiple_of(start + t * stride, 8)
                some_q[j, pl.ds((r * 3 + t) * 8, 8), :] = every_q[pl.ds(row, 8), :]
    for j in range(5):
        q = jnp.dot(order, some_q[j].astype(BF16), preferred_element_type=F32).astype(BF16)
        at = pl.multiple_of(block_ref[j] * 128, 128)
        k = met_ref[:, pl.ds(at, 128), :].reshape(1024, 128)
        v = met_ref[:, pl.ds(384 + at, 128), :].reshape(1024, 128)
        s = lax.dot_general(q, k, (((1,), (1,)), ((), ())), preferred_element_type=F32)
        seen = lax.broadcasted_iota(jnp.int32, s.shape, 1) < limit_ref[j]
        s = jnp.where(seen, s * (math.log2(math.e) / math.sqrt(128)), MASKED)
        top = jnp.max(s, axis=-1, keepdims=True)
        p = jnp.exp2(s - top)
        total = jnp.sum(p, axis=-1, keepdims=True)
        hi = p.astype(BF16)
        lo = (p - hi.astype(F32)).astype(BF16)
        o = jnp.dot(hi, v, preferred_element_type=F32)
        o = o + jnp.dot(lo, v, preferred_element_type=F32)
        some = limit_ref[j] > 0
        o = o / total
        low, high = o[:96], o[96:]
        for h, a in enumerate((jnp.concatenate([low[:, :64], high[:, :64]], axis=1),
                               jnp.concatenate([low[:, 64:], high[:, 64:]], axis=1))):
            for g in range(8):
                o_ref[2 * g + h, pl.ds(j * 12, 12), :] = a[g * 12:g * 12 + 12]
        lse = jnp.where(some, top * math.log(2.0) + jnp.log(total), ABSENT)
        spread = jnp.where(lanes == lane_of + j * 12, lse, 0.0)
        every_lse = every_lse + jnp.dot(heads_ref[...], spread, precision=HIGHEST, preferred_element_type=F32)
    a = every_lse.astype(BF16).astype(F32)
    rest = every_lse - a
    b = rest.astype(BF16).astype(F32)
    c = (rest - b).astype(BF16).astype(F32)
    for g in range(8):
        for h in range(2):
            o_ref[2 * g + h, 60:64, :] = jnp.concatenate(
                [a[g:g + 1], b[g:g + 1], c[g:g + 1], jnp.zeros((1, 128), F32)], axis=0)


def combine_kernel(got_ref, out_ref):
    lse = got_ref[:, 60, :] + got_ref[:, 61, :] + got_ref[:, 62, :]
    top = jnp.max(lse, axis=0, keepdims=True)
    w = jnp.exp(lse - top)
    total = jnp.sum(w, axis=0, keepdims=True)
    w = jnp.concatenate([w / total, jnp.zeros((112, 128), F32)], axis=0).T
    left = lax.broadcasted_iota(jnp.int32, (64, 128), 1) < 64
    o = jnp.zeros((64, 128), F32)
    for i in range(16):
        o = o + got_ref[i] * jnp.where(left, w[:64, i:i + 1], w[64:, i:i + 1])
    o = jnp.concatenate([o[:56], o[56:60], top + jnp.log(total), jnp.zeros((3, 128), F32)], axis=0)
    for i in range(4):
        out_ref[i] = o


def finish_kernel(every_ref, own_ref, num_ref, out_ref):
    flat = every_ref[...].reshape(256, 128)
    own = own_ref[...].T
    place = own[:, 0:1].astype(jnp.int32)
    lane = own[:, 1:2].astype(jnp.int32)
    half = own[:, 2:3]
    columns = lax.broadcasted_iota(jnp.int32, (128, 256), 1)
    pick = jnp.where(columns == place, 1.0, 0.0).astype(BF16)
    hi = flat.astype(BF16)
    lo = (flat - hi.astype(F32)).astype(BF16)
    o = jnp.dot(pick, hi, preferred_element_type=F32) + jnp.dot(pick, lo, preferred_element_type=F32)
    o = jnp.where(half == 0.0, o[:, :64], o[:, 64:])
    lanes = lax.broadcasted_iota(jnp.int32, (128, 128), 1)
    kept = jnp.zeros((128, 128), F32)
    for y in range(4):
        kept = jnp.where(lanes + y * 128 == lane, flat[y * 64 + 60:y * 64 + 61], kept)
    lse = jnp.sum(kept, axis=1, keepdims=True)
    own_top, den, living = own[:, 3:4], own[:, 4:5], own[:, 5:6]
    top = jnp.maximum(lse, own_top)
    a = jnp.exp(lse - top)
    b = jnp.exp(own_top - top)
    out = (a * o + b * num_ref[...]) / (a + b * den)
    out = jnp.where(living > 0.0, out, 0.0)
    out = jnp.concatenate([out[:64], out[64:]], axis=1).astype(BF16)
    for i in range(16):
        out_ref[i] = out


def lay(ref, to_ref, first):
    for g in range(8):
        left, right = ref[2 * g].astype(F32), ref[2 * g + 1].astype(F32)
        for k in range(2):
            cut = slice(k * 64, k * 64 + 64)
            rows = jnp.concatenate([left[:, cut], right[:, cut]], axis=1)
            for t in range(3):
                to_ref[t * 40 + k * 20:t * 40 + k * 20 + 20, first + g, :] = rows[t * 20:t * 20 + 20]


def own_lay_kernel(mine_ref, out_ref):
    lay(mine_ref, out_ref, 0)


def final_kernel(core_ref, mine_ref, other_ref, out_ref, whole):
    for core in range(2):
        @pl.when(core_ref[0] == core)
        def _():
            whole[:, core * 8:core * 8 + 8, :] = mine_ref[...]
            lay(other_ref, whole, 8 - core * 8)
    out_ref[...] = whole[...].reshape(3, 40, 16, 128).astype(BF16)


def shards(
    queries, prefix_keys, prefix_values, suffix_keys, suffix_values,
    new_keys, new_values, prompt_lengths, unfinished, slot_sample,
):
    steps, slots, heads, width = queries.shape
    prompts, span, key_heads, _ = prefix_keys.shape
    group = heads // key_heads
    scale = 1.0 / math.sqrt(width)
    pr = lax.axis_index("prompt")
    z, c = pr // 2, pr % 2
    y = lax.axis_index("sample")
    t_ids = jnp.arange(steps, dtype=jnp.int32)
    near = [list(range(8 * i, 8 * i + 8)) for i in range(16)]
    same_core = [[2 * i + k for i in range(16)] for k in range(2)]

    sent, mode = pl.pallas_call(
        send_kernel,
        in_specs=[SMEM, SMEM, SMEM, VMEM, HBM, HBM, HBM],
        out_specs=[HBM, SMEM],
        out_shape=[jax.ShapeDtypeStruct((8, 1008, 128), BF16), jax.ShapeDtypeStruct((1,), jnp.int32)],
        scratch_shapes=[
            pltpu.VMEM((2560, 128), BF16),
            pltpu.VMEM((2560, 128), BF16),
            pltpu.VMEM((3, 40, 16, 128), BF16),
            pltpu.VMEM((2, 4, 240, 128), F32),
            pltpu.VMEM((8, 1008, 128), BF16),
            pltpu.SMEM((48,), jnp.int32),
            pltpu.SemaphoreType.DMA((5,)),
            pltpu.SemaphoreType.DMA((24,)),
        ],
        compiler_params=pltpu.CompilerParams(vmem_limit_bytes=60 * 1024 * 1024),
    )(c.reshape(1).astype(jnp.int32), y.reshape(1).astype(jnp.int32), slot_sample, slot_sample.reshape(1, 160),
      prefix_keys.reshape(2560, width), prefix_values.reshape(2560, width), queries)
    met = lax.all_to_all(sent, ("prompt", "sample"), 0, 0, axis_index_groups=near, tiled=True)

    ids = jnp.arange(160, dtype=jnp.int32)
    wanted = y * slots + jnp.arange(slots, dtype=jnp.int32)
    slot_of = jnp.sum(jnp.where(slot_sample[None, :] == wanted[:, None], ids[None, :], 0), axis=1)
    at, from_row = slot_of % slots, slot_of // slots
    owner = slot_sample // slots
    ahead = (ids // slots == from_row[:, None]) & (ids < slot_of[:, None]) & (owner == y)
    rank = jnp.sum(ahead.astype(jnp.int32), axis=1)
    many = mode[0] > 0
    start = jnp.where(
        many,
        ((at // 20) * 4 + from_row) * 480 + (at % 20) * 8,
        ((rank % 2) * 4 + from_row) * 240 + (rank // 2) * 8,
    )

    def all_queries():
        half = lax.dynamic_slice_in_dim(queries, c * (slots // 2), slots // 2, 1)
        half = half.reshape(steps, slots // 2, key_heads, group, width)
        half = jnp.transpose(half, (2, 0, 1, 3, 4)).reshape(2, 1, 480, width)
        half = jnp.broadcast_to(half, (2, 4, 480, width)).reshape(8, 480, width)
        half = lax.all_to_all(half, ("prompt", "sample"), 0, 0, axis_index_groups=near, tiled=True)
        return half.reshape(3840, width)


    extra = lax.cond(many, all_queries, lambda: jnp.zeros((3840, width), BF16))

    odd = y % 2
    block = jnp.where(odd == 0, jnp.array([0, 0, 1, 1, 2], jnp.int32), jnp.array([0, 1, 1, 2, 2], jnp.int32))
    limit = jnp.take(prompt_lengths, (y * 5) // 2 + block) - z * 1024
    n = np.arange(192)
    order = np.zeros((192, 192), np.float32)
    order[n, ((n // 96) * 12 + n % 12) * 8 + (n % 96) // 12] = 1.0
    def rows(a):
        a = jnp.broadcast_to(a, (steps, slots) + a.shape[2:])
        a = a.reshape((steps, 2, 20) + a.shape[2:])
        a = jnp.swapaxes(a, 0, 1).reshape((2, 60) + a.shape[3:])
        return jnp.pad(a, [(0, 0), (0, 4)] + [(0, 0)] * (a.ndim - 2)).reshape((128,) + a.shape[2:])

    own_id = lax.dynamic_slice_in_dim(slot_sample, y * slots, slots, 0)
    from_y = (own_id // slots)[None, :]
    r = own_id % slots
    half = ((r % 8) // 4)[None, :]
    row = ((r // 8) * 12 + (r % 4) * 3)[None, :] + t_ids[:, None]
    going = jnp.take(unfinished, own_id // SAMPLES, axis=1)
    living = (own_id % SAMPLES)[None, :] < going
    place, lane = from_y * 64 + row, from_y * 128 + half * 64 + row

    qs = queries.reshape(steps, slots, key_heads, group, width)
    qs = lax.dynamic_slice(qs, (0, 0, c, z // 2, 0), (steps, slots, 1, 1, width))[:, :, 0, 0].astype(F32)

    def of_head(old, new, first, size):
        a = jnp.concatenate([old, jnp.swapaxes(new, 0, 1)], axis=1)
        return lax.dynamic_slice(a, (0, 0, c, first), a.shape[:2] + (1, size))[:, :, 0].astype(F32)

    keys = of_head(suffix_keys, new_keys, 0, width)
    values = of_head(suffix_values, new_values, (z % 2) * 64, 64)
    score = jnp.sum(qs[:, :, None] * keys[None], axis=-1) * scale
    u_ids = jnp.arange(keys.shape[1], dtype=jnp.int32)
    seen = (u_ids[None, :] <= suffix_keys.shape[1] + t_ids[:, None])[:, None, :]
    score = jnp.where(seen, score, MASKED)
    own_top = jnp.max(score, axis=2)
    weight = jnp.where(seen, jnp.exp(score - own_top[:, :, None]), 0.0)
    den = jnp.sum(weight, axis=2)
    num = jnp.sum(weight[..., None] * values[None], axis=2)
    own = jnp.stack([jnp.broadcast_to(a, (steps, slots)).astype(F32) for a in (place, lane, half, own_top, den, living)])
    own = jnp.swapaxes(own.reshape(6, steps, 2, 20), 1, 2).reshape(6, 2, 60)
    own = jnp.pad(own, ((0, 2), (0, 0), (0, 4))).reshape(8, 128)
    met, own, num, extra = lax.optimization_barrier((met, own, rows(num), extra))

    of_heads = np.zeros((8, 192), np.float32)
    of_heads[(n % 96) // 12, n] = 1.0
    part = pl.pallas_call(
        attend_kernel,
        in_specs=[SMEM, SMEM, SMEM, SMEM, VMEM, VMEM, VMEM, HBM],
        out_specs=VMEM,
        out_shape=jax.ShapeDtypeStruct((16, 64, 128), F32),
        scratch_shapes=[
            pltpu.VMEM((3840, 128), F32),
            pltpu.VMEM((5, 192, 128), F32),
            pltpu.VMEM((3840, 128), BF16),
            pltpu.SemaphoreType.DMA,
        ],
        compiler_params=PARAMS,
    )(many.astype(jnp.int32).reshape(1), block, limit, start, met, jnp.asarray(order, BF16), jnp.asarray(of_heads, F32), extra)

    got = lax.all_to_all(part.astype(jnp.float16), "prompt", 0, 0, axis_index_groups=same_core, tiled=True)

    part = pl.pallas_call(
        combine_kernel,
        in_specs=[VMEM],
        out_specs=VMEM,
        out_shape=jax.ShapeDtypeStruct((4, 64, 128), F32),
        compiler_params=PARAMS,
    )(got.astype(F32))
    every = lax.all_to_all(part, "sample", 0, 0, tiled=True)
    part = pl.pallas_call(
        finish_kernel,
        in_specs=[VMEM] * 3,
        out_specs=VMEM,
        out_shape=jax.ShapeDtypeStruct((16, 64, 128), BF16),
        compiler_params=PARAMS,
    )(every, own, num)

    mine = lax.all_to_all(part, "prompt", 0, 0, axis_index_groups=same_core, tiled=True)
    other = lax.ppermute(mine, "prompt", [(i, i ^ 1) for i in range(32)])
    mine = pl.pallas_call(
        own_lay_kernel,
        in_specs=[VMEM],
        out_specs=VMEM,
        out_shape=jax.ShapeDtypeStruct((120, 8, 128), F32),
        compiler_params=PARAMS,
        cost_estimate=pl.CostEstimate(flops=1000000, bytes_accessed=1500000, transcendentals=0),
    )(mine)
    return pl.pallas_call(
        final_kernel,
        in_specs=[SMEM, VMEM, VMEM],
        out_specs=VMEM,
        out_shape=jax.ShapeDtypeStruct((steps, slots, heads, width), BF16),
        scratch_shapes=[pltpu.VMEM((120, 16, 128), F32)],
        compiler_params=PARAMS,
    )(c.reshape(1).astype(jnp.int32), mine, other)


def solution(mesh):
    in_specs = (
        P(None, "sample", "tensor", None),
        P(None, ("prompt", "sample"), "tensor", None),
        P(None, ("prompt", "sample"), "tensor", None),
        P("sample", None, "tensor", None),
        P("sample", None, "tensor", None),
        P(None, "sample", "tensor", None),
        P(None, "sample", "tensor", None),
        P(),
        P(),
        P(),
    )
    out_specs = P(None, "sample", "tensor", None)
    return jax.shard_map(shards, mesh=mesh, in_specs=in_specs, out_specs=out_specs, check_vma=False)
```

time: 1180 us -> 114 us (0.10)
  blocking collectives: 982 us -> 54.3 us
  local copies, waits for them, and re-layouts: 69.4 us -> 4.42 us
  other arithmetic: 43.7 us -> 5.54 us
  matrix products: 29.2 us -> 0 us
  starting transfers between devices: 0.04 us -> 19.3 us
  waiting for transfers between devices: 31.6 us -> 16.7 us
  between operations: 13.8 us -> 0.97 us
  Pallas kernels: 0 us -> 12.8 us
    psum x1 -> x0, blocking collectives: 492 us -> none  [shards(): lax.psum((numerator, denominator), ('prompt', 'sample'))]
    pmax x1 -> x0, blocking collectives: 490 us -> none  [shards(): row_top = lax.pmax(row_top, ('prompt', 'sample'))]
    all_to_all x0 -> x3, blocking collectives: none -> 54.3 us  [the longest x1 24.3 us: shards(): lax.all_to_all(part.astype(jnp.float16), 'prompt', 0, 0, axis_index_group...]
    dynamic_slice x62 -> x0, local copies, waits for them, and re-layouts: 45 us -> none  [the longest x40 43.9 us: shards(): lax.map(prefix_scores, (sorted_query, prefix_keys, prompt_lengths))]
    all_gather x1 -> x0, waiting for transfers between devices: 30.9 us -> none  [shards(): every_query = lax.all_gather(queries, 'sample', axis=1, tiled=True)]
    dot_general x24 -> x0, matrix products: 29.2 us -> none  [the longest x10 12.9 us: prefix_sums(): jnp.einsum('jtsgl,ljd->jtsgd', weights, value_block, preferred_element_ty...]
    all_to_all x0 -> x1, waiting for transfers between devices: none -> 15.9 us  [shards(): lax.all_to_all(sent, ('prompt', 'sample'), 0, 0, axis_index_groups=near,...]
    pallas_call x0 -> x6, Pallas kernels: none -> 12.8 us  [the longest x1 5.42 us: shards(): pl.pallas_call(send_kernel, in_specs=[SMEM, SMEM, SMEM, VMEM, HBM, HBM, H...]
  transfers between devices with their start and end apart: 2 -> 2, of which waited for: 1 -> 2; matrix products, arithmetic and copies ran while one was open for 2% -> 9% of each run, Pallas kernels for 0% -> 0%
where the time goes in v1:
time: 114 us
  blocking collectives  54.3 us (48%)
  starting transfers between devices  19.3 us (17%)
  waiting for transfers between devices  16.7 us (15%)
  Pallas kernels  12.8 us (11%)
  other arithmetic  5.54 us (5%)
  local copies, waits for them, and re-layouts  4.42 us (4%)
    all_to_all x1, blocking collectives, shards(): lax.all_to_all(part.astype(jnp.float16), 'prompt', 0, 0, axis_index_group...  24.3 us
    all_to_all x1, blocking collectives, shards(): lax.all_to_all(part, 'prompt', 0, 0, axis_index_groups=same_core, tiled=T...  22.8 us
    all_to_all x1, waiting for transfers between devices, shards(): lax.all_to_all(sent, ('prompt', 'sample'), 0, 0, axis_index_groups=near,...  15.9 us
    all_to_all x1, starting transfers between devices, shards(): lax.all_to_all(sent, ('prompt', 'sample'), 0, 0, axis_index_groups=near,...  10.5 us
    ppermute x1, starting transfers between devices, shards(): other = lax.ppermute(mine, 'prompt', [(i, i ^ 1) for i in range(32)])  8.76 us
    all_to_all x1, blocking collectives, shards(): every = lax.all_to_all(part, 'sample', 0, 0, tiled=True)  7.21 us
    pallas_call x1, Pallas kernels, shards(): pl.pallas_call(send_kernel, in_specs=[SMEM, SMEM, SMEM, VMEM, HBM, HBM, H...  5.42 us
    pallas_call x1, Pallas kernels, shards(): pl.pallas_call(attend_kernel, in_specs=[SMEM, SMEM, SMEM, SMEM, VMEM, VME...  4.66 us
  transfers between devices with their start and end apart: 2, of which 2 were waited for; matrix products, arithmetic and copies ran while one was open for 9% of the time, Pallas kernels for 0%

profile of v1, /device:TPU:1, one launch (start us, length us, event | category | flops | bytes accessed | tf_op | source)
XLA Modules:
  0.0 114.0 jit_solution(3534576721837607415)
XLA Ops:
  0.0 5.4 %shard_map.136 = (bf16[8,1008,128]{2,1,0:T(8,128)(2,1)}, s32[1]{0:T(128)}) custom-call(s32[1]{0:T(128)} %bitcast.6.core_ref, s32[1]{0:T(128)} %bitcast.7.row_ref, s32[160]{0:T(256)} %slot_ref.1, s32[1,160]{1,0:T(1,128)} %bitcast.51, bf16[2560,128]{1,0:T(8,128)(2,1)} %bitcast.42, bf16[2560,128]{1,0:T(8,128)(2,1)} %bitcast.43, bf16[3,40,16,128]{3,2,1,0:T(8,128)(2,1)} %q_hbm.1), custom_call_target="tpu_custom_call" | custom-call | tf_op jit(solution)/shard_map/pallas_call | solution.py:233
  6.1 0.1 conditional.1
  6.1 0.1 broadcast.257
  6.2 0.0 copy-start.3
  6.2 0.0 copy-start.5
  6.2 0.0 copy-start.6
  6.3 10.5 %all-to-all-start.1 = ((bf16[8,1008,128]{2,1,0:T(8,128)(2,1)}), bf16[8,1008,128]{2,1,0:T(8,128)(2,1)S(1)}, u32[]{:S(2)}, u32[]{:S(2)}) async-start(bf16[8,1008,128]{2,1,0:T(8,128)(2,1)} %get-tuple-element.21), calls=%async_computation.1 | async-start | bytes 4128768 | tf_op jit(solution)/shard_map/all_to_all | solution.py:251
  16.8 0.5 iota_add_fusion.2
  17.3 0.6 iota_add_fusion.1
  18.0 0.7 iota_compare_fusion.1
  18.7 1.0 dynamic-slice_convert_fusion
  19.7 0.2 multiply_reduce_fusion.1
  20.0 0.1 fusion.8
  20.1 0.1 stack.19
  20.2 0.1 fusion.15
  20.3 0.8 select_reduce_fusion
  21.0 0.1 and_select_fusion.1
  21.2 0.1 add.222
  21.3 0.1 add.217
  21.4 0.1 add.229
  21.5 0.1 stack.17
  21.6 0.1 stack.20
  21.6 0.1 copy.47
  21.7 0.6 gather_fusion.1
  22.3 0.1 copy.48
  22.4 0.1 gather.12
  22.5 0.1 broadcast_in_dim.90
  22.6 0.1 lt.115
  22.7 0.1 reshape.281
  22.8 0.1 reshape.282.own_ref
  22.9 1.0 copy.51
  23.9 0.8 copy.59
  24.7 0.1 fusion.2
  24.8 0.2 multiply_reduce_fusion
  25.2 0.7 compare_select_fusion.1
  25.9 0.6 gather_fusion
  26.6 0.2 convert_reduce_fusion
  26.8 15.9 %all-to-all-done.1.met_ref = bf16[8,1008,128]{2,1,0:T(8,128)(2,1)S(1)} async-done(((bf16[8,1008,128]{2,1,0:T(8,128)(2,1)}), bf16[8,1008,128]{2,1,0:T(8,128)(2,1)S(1)}, u32[]{:S(2)}, u32[]{:S(2)}) %all-to-all-start.1) | async-done | bytes 2064416 | tf_op jit(solution)/shard_map/all_to_all | solution.py:251
  42.7 4.7 %shard_map.137 = f32[16,64,128]{2,1,0:T(8,128)S(1)} custom-call(s32[1]{0:T(128)} %bitcast.12.mode_ref, s32[5]{0:T(128)S(1)} %get-tuple-element.38.block_ref, s32[5]{0:T(128)S(1)} %fusion.14.limit_ref, s32[40]{0:T(128)S(1)} %broadcast_select_fusion.start_ref, bf16[8,1008,128]{2,1,0:T(8,128)(2,1)S(1)} %all-to-all-done.1.met_ref, ...), custom_call_target="tpu_custom_call" | custom-call | tf_op jit(solution)/shard_map/pallas_call | solution.py:323
  47.4 24.3 %all_to_all.25 = f16[16,64,128]{2,1,0:T(8,128)(2,1)S(1)} all-to-all(f16[16,64,128]{2,1,0:T(8,128)(2,1)S(1)} %convert_element_type.96), channel_id=1, replica_groups={{0,32,64,96,128,160,192,224,256,288,320,352,384,416,448,480},{16,48,80,..., dimensions={0} | all-to-all | bytes 524288 | tf_op jit(solution)/shard_map/all_to_all | solution.py:337
  71.8 0.5 shard_map.138
  72.3 7.2 %all_to_all.26.every_ref = f32[4,64,128]{2,1,0:T(8,128)S(1)} all-to-all(f32[4,64,128]{2,1,0:T(8,128)S(1)} %shard_map.138), channel_id=1, replica_groups=mesh['prompt'=32,'sample'=4,'tensor'=4] {'sample'}, dimensions={0} | all-to-all | bytes 262144 | tf_op jit(solution)/shard_map/all_to_all | solution.py:346
  79.5 0.6 shard_map.139
  80.1 22.8 %all_to_all.27.mine_ref = bf16[16,64,128]{2,1,0:T(8,128)(2,1)S(1)} all-to-all(bf16[16,64,128]{2,1,0:T(8,128)(2,1)S(1)} %shard_map.139), channel_id=1, replica_groups={{0,32,64,96,128,160,192,224,256,288,320,352,384,416,448,480},{16,48,80,..., dimensions={0} | all-to-all | bytes 524288 | tf_op jit(solution)/shard_map/all_to_all | solution.py:355
  102.9 8.8 %collective-permute-start = (bf16[16,64,128]{2,1,0:T(8,128)(2,1)S(1)}, bf16[16,64,128]{2,1,0:T(8,128)(2,1)S(1)}, u32[]{:S(2)}, u32[]{:S(2)}) collective-permute-start(bf16[16,64,128]{2,1,0:T(8,128)(2,1)S(1)} %all_to_all.27.mine_ref), channel_id=1, source_target_pairs={{0,16},{16,0},{32,48},{48,32},{64,80},{80,64},{96,112},{112,96},{1... | collective-permute-start | bytes 786440 | tf_op jit(solution)/shard_map/ppermute | solution.py:356
  111.6 0.3 shard_map.140.mine_ref
  112.0 0.8 collective-permute-done.other_ref
  112.8 1.2 %shard_map.141 = bf16[3,40,16,128]{3,2,1,0:T(8,128)(2,1)} custom-call(s32[1]{0:T(128)} %bitcast.6.core_ref, f32[120,8,128]{2,1,0:T(8,128)S(1)} %shard_map.140.mine_ref, bf16[16,64,128]{2,1,0:T(8,128)(2,1)S(1)} %collective-permute-done.other_ref), custom_call_target="tpu_custom_call" | custom-call | tf_op jit(solution)/shard_map/pallas_call | solution.py:365
  (39 shorter events, 0.5 us)
Async XLA Ops:
  0.0 25.9 %copy-start = (s32[10]{0:T(128)S(1)}, s32[10]{0:T(128)}, u32[]{:S(2)}) copy-start(s32[10]{0:T(128)} %param.23) | copy-start | bytes 124
  6.2 11.7 %copy-start.3 = (bf16[40,8,2,128]{3,2,1,0:T(2,128)(2,1)S(1)}, bf16[40,8,2,128]{3,2,1,0:T(2,128)(2,1)}, u32[]{:S(2)}) copy-start(bf16[40,8,2,128]{3,2,1,0:T(2,128)(2,1)} %param.19) | copy-start | bytes 491524
  6.2 11.7 %copy-start.4 = (bf16[3,40,2,128]{3,2,1,0:T(2,128)(2,1)S(1)}, bf16[3,40,2,128]{3,2,1,0:T(2,128)(2,1)}, u32[]{:S(2)}) copy-start(bf16[3,40,2,128]{3,2,1,0:T(2,128)(2,1)} %param.21) | copy-start | bytes 184324
  6.2 14.0 %copy-start.5 = (s32[160]{0:T(256)S(1)}, s32[160]{0:T(256)}, u32[]{:S(2)}) copy-start(s32[160]{0:T(256)} %slot_ref.1) | copy-start | bytes 1924
  6.2 15.4 %copy-start.6 = (s32[3,10]{1,0:T(4,128)S(1)}, s32[3,10]{1,0:T(4,128)}, u32[]{:S(2)}) copy-start(s32[3,10]{1,0:T(4,128)} %param.24) | copy-start | bytes 364
  6.3 36.4 %all-to-all-start.1 = ((bf16[8,1008,128]{2,1,0:T(8,128)(2,1)}), bf16[8,1008,128]{2,1,0:T(8,128)(2,1)S(1)}, u32[]{:S(2)}, u32[]{:S(2)}) async-start(bf16[8,1008,128]{2,1,0:T(8,128)(2,1)} %get-tuple-element.21), calls=%async_computation.1 | async-start | bytes 4128768 | tf_op jit(solution)/shard_map/all_to_all | solution.py:251
  16.8 25.9 %copy-start.1 = (bf16[192,192]{1,0:T(8,128)(2,1)S(1)}, bf16[192,192]{1,0:T(8,128)(2,1)}, u32[]{:S(2)}) copy-start(bf16[192,192]{1,0:T(8,128)(2,1)} %constant.248.clone.order_ref) | copy-start | bytes 221188
  16.8 25.9 %copy-start.2 = (f32[8,192]{1,0:T(8,128)S(1)}, f32[8,192]{1,0:T(8,128)}, u32[]{:S(2)}) copy-start(f32[8,192]{1,0:T(8,128)} %constant.249.clone.heads_ref) | copy-start | bytes 18436
  102.9 9.9 %collective-permute-start = (bf16[16,64,128]{2,1,0:T(8,128)(2,1)S(1)}, bf16[16,64,128]{2,1,0:T(8,128)(2,1)S(1)}, u32[]{:S(2)}, u32[]{:S(2)}) collective-permute-start(bf16[16,64,128]{2,1,0:T(8,128)(2,1)S(1)} %all_to_all.27.mine_ref), channel_id=1, source_target_pairs={{0,16},{16,0},{32,48},{48,32},{64,80},{80,64},{96,112},{112,96},{1... | collective-permute-start | bytes 786440 | tf_op jit(solution)/shard_map/ppermute | solution.py:356

commit v2 on v1

--- a/solution.py
+++ b/solution.py
@@ -25,7 +25,7 @@
 
 
 def send_kernel(core_ref, row_ref, slot_ref, slots_ref, k_hbm, v_hbm, q_hbm, out_hbm, mode_ref,
-                k_ref, v_ref, q_ref, some_q, out_ref, list_ref, in_sem, out_sem):
+                k_ref, v_ref, q_ref, some_q, out_ref, list_ref, count_ref, in_sem, out_sem):
     ins = []
     for n, (src, dst) in enumerate(((k_hbm, k_ref), (v_hbm, v_ref))):
         for i in range(2):
@@ -37,14 +37,21 @@
     outs = []
     for i in range(40):
         list_ref[i] = 0
-    counts = [jnp.int32(0)] * 4
-    for i in range(40):
+    for i in range(4):
+        count_ref[i] = 0
+
+    def note(i, _):
         sample = slot_ref[row_ref[0] * 40 + i]
         to = (sample >= 40).astype(jnp.int32) + (sample >= 80).astype(jnp.int32) + (sample >= 120).astype(jnp.int32)
-        n = jnp.where(to < 2, jnp.where(to == 0, counts[0], counts[1]), jnp.where(to == 2, counts[2], counts[3]))
-        counts = [counts[k] + (to == k).astype(jnp.int32) for k in range(4)]
-        mine = ((n & 1) == core_ref[0]) & (n < 20)
-        list_ref[jnp.where(mine, to * 10 + (n >> 1), 40)] = i
+        n = count_ref[to]
+        count_ref[to] = n + 1
+
+        @pl.when(((n & 1) == core_ref[0]) & (n < 20))
+        def _():
+            list_ref[to * 10 + (n >> 1)] = i
+        return 0
+
+    lax.fori_loop(0, 40, note, 0)
 
     def quarter(a):
         return (a >= 40).astype(jnp.int32) + (a >= 80).astype(jnp.int32) + (a >= 120).astype(jnp.int32)
@@ -241,7 +248,8 @@
             pltpu.VMEM((3, 40, 16, 128), BF16),
             pltpu.VMEM((2, 4, 240, 128), F32),
             pltpu.VMEM((8, 1008, 128), BF16),
-            pltpu.SMEM((48,), jnp.int32),
+            pltpu.SMEM((40,), jnp.int32),
+            pltpu.SMEM((4,), jnp.int32),
             pltpu.SemaphoreType.DMA((5,)),
             pltpu.SemaphoreType.DMA((24,)),
         ],

time: 114 us -> 114 us (level)
  no operation moved by 1% of the time
where the time goes in v2:
time: 114 us
  blocking collectives  54.3 us (48%)
  starting transfers between devices  19.3 us (17%)
  waiting for transfers between devices  16.7 us (15%)
  Pallas kernels  12.4 us (11%)
  other arithmetic  5.54 us (5%)
  local copies, waits for them, and re-layouts  4.42 us (4%)
    all_to_all x1, blocking collectives, shards(): lax.all_to_all(part.astype(jnp.float16), 'prompt', 0, 0, axis_index_group...  24.3 us
    all_to_all x1, blocking collectives, shards(): lax.all_to_all(part, 'prompt', 0, 0, axis_index_groups=same_core, tiled=T...  22.8 us
    all_to_all x1, waiting for transfers between devices, shards(): lax.all_to_all(sent, ('prompt', 'sample'), 0, 0, axis_index_groups=near,...  15.9 us
    all_to_all x1, starting transfers between devices, shards(): lax.all_to_all(sent, ('prompt', 'sample'), 0, 0, axis_index_groups=near,...  10.5 us
    ppermute x1, starting transfers between devices, shards(): other = lax.ppermute(mine, 'prompt', [(i, i ^ 1) for i in range(32)])  8.76 us
    all_to_all x1, blocking collectives, shards(): every = lax.all_to_all(part, 'sample', 0, 0, tiled=True)  7.21 us
    pallas_call x1, Pallas kernels, shards(): pl.pallas_call(send_kernel, in_specs=[SMEM, SMEM, SMEM, VMEM, HBM, HBM, H...  5.05 us
    pallas_call x1, Pallas kernels, shards(): pl.pallas_call(attend_kernel, in_specs=[SMEM, SMEM, SMEM, SMEM, VMEM, VME...  4.66 us
  transfers between devices with their start and end apart: 2, of which 2 were waited for; matrix products, arithmetic and copies ran while one was open for 9% of the time, Pallas kernels for 0%

profile of v2, /device:TPU:1, one launch (start us, length us, event | category | flops | bytes accessed | tf_op | source)
XLA Modules:
  0.0 113.6 jit_solution(13798625482190734707)
XLA Ops:
  0.0 5.0 %shard_map.136 = (bf16[8,1008,128]{2,1,0:T(8,128)(2,1)}, s32[1]{0:T(128)}) custom-call(s32[1]{0:T(128)} %bitcast.6.core_ref, s32[1]{0:T(128)} %bitcast.7.row_ref, s32[160]{0:T(256)} %slot_ref.1, s32[1,160]{1,0:T(1,128)} %bitcast.51, bf16[2560,128]{1,0:T(8,128)(2,1)} %bitcast.42, bf16[2560,128]{1,0:T(8,128)(2,1)} %bitcast.43, bf16[3,40,16,128]{3,2,1,0:T(8,128)(2,1)} %q_hbm.1), custom_call_target="tpu_custom_call" | custom-call | tf_op jit(solution)/shard_map/pallas_call | solution.py:240
  5.7 0.1 conditional.1
  5.7 0.1 broadcast.257
  5.8 0.0 copy-start.3
  5.8 0.0 copy-start.4
  5.9 0.0 copy-start.5
  5.9 10.5 %all-to-all-start.1 = ((bf16[8,1008,128]{2,1,0:T(8,128)(2,1)}), bf16[8,1008,128]{2,1,0:T(8,128)(2,1)S(1)}, u32[]{:S(2)}, u32[]{:S(2)}) async-start(bf16[8,1008,128]{2,1,0:T(8,128)(2,1)} %get-tuple-element.21), calls=%async_computation.1 | async-start | bytes 4128768 | tf_op jit(solution)/shard_map/all_to_all | solution.py:259
  16.4 0.5 iota_add_fusion.2
  16.9 0.6 iota_add_fusion.1
  17.6 0.7 iota_compare_fusion.1
  18.3 1.0 dynamic-slice_convert_fusion
  19.3 0.2 multiply_reduce_fusion.1
  19.6 0.1 fusion.8
  19.7 0.1 stack.19
  19.8 0.1 fusion.15
  19.9 0.8 select_reduce_fusion
  20.6 0.1 and_select_fusion.1
  20.8 0.1 add.222
  20.9 0.1 add.217
  21.0 0.1 add.229
  21.1 0.1 stack.17
  21.2 0.1 stack.20
  21.3 0.1 copy.47
  21.4 0.6 gather_fusion.1
  21.9 0.1 copy.48
  22.0 0.1 gather.12
  22.1 0.1 broadcast_in_dim.90
  22.2 0.1 lt.115
  22.4 0.1 reshape.281
  22.5 0.1 reshape.282.own_ref
  22.5 1.0 copy.51
  23.5 0.8 copy.59
  24.3 0.1 fusion.2
  24.5 0.2 multiply_reduce_fusion
  24.8 0.7 compare_select_fusion.1
  25.5 0.6 gather_fusion
  26.2 0.2 convert_reduce_fusion
  26.4 15.9 %all-to-all-done.1.met_ref = bf16[8,1008,128]{2,1,0:T(8,128)(2,1)S(1)} async-done(((bf16[8,1008,128]{2,1,0:T(8,128)(2,1)}), bf16[8,1008,128]{2,1,0:T(8,128)(2,1)S(1)}, u32[]{:S(2)}, u32[]{:S(2)}) %all-to-all-start.1) | async-done | bytes 2064416 | tf_op jit(solution)/shard_map/all_to_all | solution.py:259
  42.3 4.7 %shard_map.137 = f32[16,64,128]{2,1,0:T(8,128)S(1)} custom-call(s32[1]{0:T(128)} %bitcast.12.mode_ref, s32[5]{0:T(128)S(1)} %get-tuple-element.38.block_ref, s32[5]{0:T(128)S(1)} %fusion.14.limit_ref, s32[40]{0:T(128)S(1)} %broadcast_select_fusion.start_ref, bf16[8,1008,128]{2,1,0:T(8,128)(2,1)S(1)} %all-to-all-done.1.met_ref, ...), custom_call_target="tpu_custom_call" | custom-call | tf_op jit(solution)/shard_map/pallas_call | solution.py:331
  47.0 24.3 %all_to_all.25 = f16[16,64,128]{2,1,0:T(8,128)(2,1)S(1)} all-to-all(f16[16,64,128]{2,1,0:T(8,128)(2,1)S(1)} %convert_element_type.96), channel_id=1, replica_groups={{0,32,64,96,128,160,192,224,256,288,320,352,384,416,448,480},{16,48,80,..., dimensions={0} | all-to-all | bytes 524288 | tf_op jit(solution)/shard_map/all_to_all | solution.py:345
  71.4 0.5 shard_map.138
  71.9 7.2 %all_to_all.26.every_ref = f32[4,64,128]{2,1,0:T(8,128)S(1)} all-to-all(f32[4,64,128]{2,1,0:T(8,128)S(1)} %shard_map.138), channel_id=1, replica_groups=mesh['prompt'=32,'sample'=4,'tensor'=4] {'sample'}, dimensions={0} | all-to-all | bytes 262144 | tf_op jit(solution)/shard_map/all_to_all | solution.py:354
  79.1 0.6 shard_map.139
  79.7 22.8 %all_to_all.27.mine_ref = bf16[16,64,128]{2,1,0:T(8,128)(2,1)S(1)} all-to-all(bf16[16,64,128]{2,1,0:T(8,128)(2,1)S(1)} %shard_map.139), channel_id=1, replica_groups={{0,32,64,96,128,160,192,224,256,288,320,352,384,416,448,480},{16,48,80,..., dimensions={0} | all-to-all | bytes 524288 | tf_op jit(solution)/shard_map/all_to_all | solution.py:363
  102.5 8.8 %collective-permute-start = (bf16[16,64,128]{2,1,0:T(8,128)(2,1)S(1)}, bf16[16,64,128]{2,1,0:T(8,128)(2,1)S(1)}, u32[]{:S(2)}, u32[]{:S(2)}) collective-permute-start(bf16[16,64,128]{2,1,0:T(8,128)(2,1)S(1)} %all_to_all.27.mine_ref), channel_id=1, source_target_pairs={{0,16},{16,0},{32,48},{48,32},{64,80},{80,64},{96,112},{112,96},{1... | collective-permute-start | bytes 786440 | tf_op jit(solution)/shard_map/ppermute | solution.py:364
  111.2 0.3 shard_map.140.mine_ref
  111.6 0.8 collective-permute-done.other_ref
  112.4 1.2 %shard_map.141 = bf16[3,40,16,128]{3,2,1,0:T(8,128)(2,1)} custom-call(s32[1]{0:T(128)} %bitcast.6.core_ref, f32[120,8,128]{2,1,0:T(8,128)S(1)} %shard_map.140.mine_ref, bf16[16,64,128]{2,1,0:T(8,128)(2,1)S(1)} %collective-permute-done.other_ref), custom_call_target="tpu_custom_call" | custom-call | tf_op jit(solution)/shard_map/pallas_call | solution.py:373
  (39 shorter events, 0.5 us)
Async XLA Ops:
  0.0 25.5 %copy-start = (s32[10]{0:T(128)S(1)}, s32[10]{0:T(128)}, u32[]{:S(2)}) copy-start(s32[10]{0:T(128)} %param.23) | copy-start | bytes 124
  5.8 11.6 %copy-start.3 = (bf16[40,8,2,128]{3,2,1,0:T(2,128)(2,1)S(1)}, bf16[40,8,2,128]{3,2,1,0:T(2,128)(2,1)}, u32[]{:S(2)}) copy-start(bf16[40,8,2,128]{3,2,1,0:T(2,128)(2,1)} %param.19) | copy-start | bytes 491524
  5.8 11.7 %copy-start.4 = (bf16[3,40,2,128]{3,2,1,0:T(2,128)(2,1)S(1)}, bf16[3,40,2,128]{3,2,1,0:T(2,128)(2,1)}, u32[]{:S(2)}) copy-start(bf16[3,40,2,128]{3,2,1,0:T(2,128)(2,1)} %param.21) | copy-start | bytes 184324
  5.9 14.0 %copy-start.5 = (s32[160]{0:T(256)S(1)}, s32[160]{0:T(256)}, u32[]{:S(2)}) copy-start(s32[160]{0:T(256)} %slot_ref.1) | copy-start | bytes 1924
  5.9 15.4 %copy-start.6 = (s32[3,10]{1,0:T(4,128)S(1)}, s32[3,10]{1,0:T(4,128)}, u32[]{:S(2)}) copy-start(s32[3,10]{1,0:T(4,128)} %param.24) | copy-start | bytes 364
  5.9 36.4 %all-to-all-start.1 = ((bf16[8,1008,128]{2,1,0:T(8,128)(2,1)}), bf16[8,1008,128]{2,1,0:T(8,128)(2,1)S(1)}, u32[]{:S(2)}, u32[]{:S(2)}) async-start(bf16[8,1008,128]{2,1,0:T(8,128)(2,1)} %get-tuple-element.21), calls=%async_computation.1 | async-start | bytes 4128768 | tf_op jit(solution)/shard_map/all_to_all | solution.py:259
  16.4 25.9 %copy-start.1 = (bf16[192,192]{1,0:T(8,128)(2,1)S(1)}, bf16[192,192]{1,0:T(8,128)(2,1)}, u32[]{:S(2)}) copy-start(bf16[192,192]{1,0:T(8,128)(2,1)} %constant.248.clone.order_ref) | copy-start | bytes 221188
  16.4 25.9 %copy-start.2 = (f32[8,192]{1,0:T(8,128)S(1)}, f32[8,192]{1,0:T(8,128)}, u32[]{:S(2)}) copy-start(f32[8,192]{1,0:T(8,128)} %constant.249.clone.heads_ref) | copy-start | bytes 18436
  102.5 9.9 %collective-permute-start = (bf16[16,64,128]{2,1,0:T(8,128)(2,1)S(1)}, bf16[16,64,128]{2,1,0:T(8,128)(2,1)S(1)}, u32[]{:S(2)}, u32[]{:S(2)}) collective-permute-start(bf16[16,64,128]{2,1,0:T(8,128)(2,1)S(1)} %all_to_all.27.mine_ref), channel_id=1, source_target_pairs={{0,16},{16,0},{32,48},{48,32},{64,80},{80,64},{96,112},{112,96},{1... | collective-permute-start | bytes 786440 | tf_op jit(solution)/shard_map/ppermute | solution.py:364

commit v3 on v2

--- a/solution.py
+++ b/solution.py
@@ -127,8 +127,8 @@
         k = met_ref[:, pl.ds(at, 128), :].reshape(1024, 128)
         v = met_ref[:, pl.ds(384 + at, 128), :].reshape(1024, 128)
         s = lax.dot_general(q, k, (((1,), (1,)), ((), ())), preferred_element_type=F32)
-        seen = lax.broadcasted_iota(jnp.int32, s.shape, 1) < limit_ref[j]
-        s = jnp.where(seen, s * (math.log2(math.e) / math.sqrt(128)), MASKED)
+        unseen = jnp.where(lax.broadcasted_iota(jnp.int32, (1, 1024), 1) < limit_ref[j], 0.0, MASKED)
+        s = s * (math.log2(math.e) / math.sqrt(128)) + unseen
         top = jnp.max(s, axis=-1, keepdims=True)
         p = jnp.exp2(s - top)
         total = jnp.sum(p, axis=-1, keepdims=True)
@@ -137,7 +137,7 @@
         o = jnp.dot(hi, v, preferred_element_type=F32)
         o = o + jnp.dot(lo, v, preferred_element_type=F32)
         some = limit_ref[j] > 0
-        o = o / total
+        o = o * (1.0 / total)
         low, high = o[:96], o[96:]
         for h, a in enumerate((jnp.concatenate([low[:, :64], high[:, :64]], axis=1),
                                jnp.concatenate([low[:, 64:], high[:, 64:]], axis=1))):

time: 114 us -> 114 us (level)
  no operation moved by 1% of the time
where the time goes in v3:
time: 114 us
  blocking collectives  54.3 us (48%)
  starting transfers between devices  19.3 us (17%)
  waiting for transfers between devices  16.7 us (15%)
  Pallas kernels  12.4 us (11%)
  other arithmetic  5.54 us (5%)
  local copies, waits for them, and re-layouts  4.42 us (4%)
    all_to_all x1, blocking collectives, shards(): lax.all_to_all(part.astype(jnp.float16), 'prompt', 0, 0, axis_index_group...  24.3 us
    all_to_all x1, blocking collectives, shards(): lax.all_to_all(part, 'prompt', 0, 0, axis_index_groups=same_core, tiled=T...  22.8 us
    all_to_all x1, waiting for transfers between devices, shards(): lax.all_to_all(sent, ('prompt', 'sample'), 0, 0, axis_index_groups=near,...  15.9 us
    all_to_all x1, starting transfers between devices, shards(): lax.all_to_all(sent, ('prompt', 'sample'), 0, 0, axis_index_groups=near,...  10.5 us
    ppermute x1, starting transfers between devices, shards(): other = lax.ppermute(mine, 'prompt', [(i, i ^ 1) for i in range(32)])  8.76 us
    all_to_all x1, blocking collectives, shards(): every = lax.all_to_all(part, 'sample', 0, 0, tiled=True)  7.21 us
    pallas_call x1, Pallas kernels, shards(): pl.pallas_call(send_kernel, in_specs=[SMEM, SMEM, SMEM, VMEM, HBM, HBM, H...  5.05 us
    pallas_call x1, Pallas kernels, shards(): pl.pallas_call(attend_kernel, in_specs=[SMEM, SMEM, SMEM, SMEM, VMEM, VME...  4.69 us
  transfers between devices with their start and end apart: 2, of which 2 were waited for; matrix products, arithmetic and copies ran while one was open for 9% of the time, Pallas kernels for 0%

profile of v3, /device:TPU:1, one launch (start us, length us, event | category | flops | bytes accessed | tf_op | source)
XLA Modules:
  0.0 113.6 jit_solution(10096535708552895391)
XLA Ops:
  0.0 5.0 %shard_map.136 = (bf16[8,1008,128]{2,1,0:T(8,128)(2,1)}, s32[1]{0:T(128)}) custom-call(s32[1]{0:T(128)} %bitcast.6.core_ref, s32[1]{0:T(128)} %bitcast.7.row_ref, s32[160]{0:T(256)} %slot_ref.1, s32[1,160]{1,0:T(1,128)} %bitcast.51, bf16[2560,128]{1,0:T(8,128)(2,1)} %bitcast.42, bf16[2560,128]{1,0:T(8,128)(2,1)} %bitcast.43, bf16[3,40,16,128]{3,2,1,0:T(8,128)(2,1)} %q_hbm.1), custom_call_target="tpu_custom_call" | custom-call | tf_op jit(solution)/shard_map/pallas_call | solution.py:240
  5.7 0.1 conditional.1
  5.7 0.1 broadcast.257
  5.8 0.0 copy-start.3
  5.9 0.0 copy-start.5
  5.9 0.0 copy-start.6
  5.9 10.5 %all-to-all-start.1 = ((bf16[8,1008,128]{2,1,0:T(8,128)(2,1)}), bf16[8,1008,128]{2,1,0:T(8,128)(2,1)S(1)}, u32[]{:S(2)}, u32[]{:S(2)}) async-start(bf16[8,1008,128]{2,1,0:T(8,128)(2,1)} %get-tuple-element.21), calls=%async_computation.1 | async-start | bytes 4128768 | tf_op jit(solution)/shard_map/all_to_all | solution.py:259
  16.4 0.5 iota_add_fusion.2
  16.9 0.6 iota_add_fusion.1
  17.6 0.7 iota_compare_fusion.1
  18.3 1.0 dynamic-slice_convert_fusion
  19.3 0.2 multiply_reduce_fusion.1
  19.6 0.1 fusion.8
  19.7 0.1 stack.19
  19.8 0.1 fusion.15
  19.9 0.8 select_reduce_fusion
  20.6 0.1 and_select_fusion.1
  20.8 0.1 add.222
  20.9 0.1 add.217
  21.0 0.1 add.229
  21.1 0.1 stack.17
  21.2 0.1 stack.20
  21.3 0.1 copy.47
  21.4 0.6 gather_fusion.1
  21.9 0.1 copy.48
  22.0 0.1 gather.12
  22.1 0.1 broadcast_in_dim.90
  22.2 0.1 lt.115
  22.4 0.1 reshape.281
  22.5 0.1 reshape.282.own_ref
  22.5 1.0 copy.51
  23.5 0.8 copy.59
  24.3 0.1 fusion.2
  24.5 0.2 multiply_reduce_fusion
  24.8 0.7 compare_select_fusion.1
  25.5 0.6 gather_fusion
  26.2 0.2 convert_reduce_fusion
  26.4 15.9 %all-to-all-done.1.met_ref = bf16[8,1008,128]{2,1,0:T(8,128)(2,1)S(1)} async-done(((bf16[8,1008,128]{2,1,0:T(8,128)(2,1)}), bf16[8,1008,128]{2,1,0:T(8,128)(2,1)S(1)}, u32[]{:S(2)}, u32[]{:S(2)}) %all-to-all-start.1) | async-done | bytes 2064416 | tf_op jit(solution)/shard_map/all_to_all | solution.py:259
  42.3 4.7 %shard_map.137 = f32[16,64,128]{2,1,0:T(8,128)S(1)} custom-call(s32[1]{0:T(128)} %bitcast.12.mode_ref, s32[5]{0:T(128)S(1)} %get-tuple-element.38.block_ref, s32[5]{0:T(128)S(1)} %fusion.14.limit_ref, s32[40]{0:T(128)S(1)} %broadcast_select_fusion.start_ref, bf16[8,1008,128]{2,1,0:T(8,128)(2,1)S(1)} %all-to-all-done.1.met_ref, ...), custom_call_target="tpu_custom_call" | custom-call | tf_op jit(solution)/shard_map/pallas_call | solution.py:331
  47.1 24.3 %all_to_all.25 = f16[16,64,128]{2,1,0:T(8,128)(2,1)S(1)} all-to-all(f16[16,64,128]{2,1,0:T(8,128)(2,1)S(1)} %convert_element_type.96), channel_id=1, replica_groups={{0,32,64,96,128,160,192,224,256,288,320,352,384,416,448,480},{16,48,80,..., dimensions={0} | all-to-all | bytes 524288 | tf_op jit(solution)/shard_map/all_to_all | solution.py:345
  71.4 0.5 shard_map.138
  72.0 7.2 %all_to_all.26.every_ref = f32[4,64,128]{2,1,0:T(8,128)S(1)} all-to-all(f32[4,64,128]{2,1,0:T(8,128)S(1)} %shard_map.138), channel_id=1, replica_groups=mesh['prompt'=32,'sample'=4,'tensor'=4] {'sample'}, dimensions={0} | all-to-all | bytes 262144 | tf_op jit(solution)/shard_map/all_to_all | solution.py:354
  79.2 0.6 shard_map.139
  79.7 22.8 %all_to_all.27.mine_ref = bf16[16,64,128]{2,1,0:T(8,128)(2,1)S(1)} all-to-all(bf16[16,64,128]{2,1,0:T(8,128)(2,1)S(1)} %shard_map.139), channel_id=1, replica_groups={{0,32,64,96,128,160,192,224,256,288,320,352,384,416,448,480},{16,48,80,..., dimensions={0} | all-to-all | bytes 524288 | tf_op jit(solution)/shard_map/all_to_all | solution.py:363
  102.5 8.8 %collective-permute-start = (bf16[16,64,128]{2,1,0:T(8,128)(2,1)S(1)}, bf16[16,64,128]{2,1,0:T(8,128)(2,1)S(1)}, u32[]{:S(2)}, u32[]{:S(2)}) collective-permute-start(bf16[16,64,128]{2,1,0:T(8,128)(2,1)S(1)} %all_to_all.27.mine_ref), channel_id=1, source_target_pairs={{0,16},{16,0},{32,48},{48,32},{64,80},{80,64},{96,112},{112,96},{1... | collective-permute-start | bytes 786440 | tf_op jit(solution)/shard_map/ppermute | solution.py:364
  111.3 0.3 shard_map.140.mine_ref
  111.6 0.8 collective-permute-done.other_ref
  112.4 1.2 %shard_map.141 = bf16[3,40,16,128]{3,2,1,0:T(8,128)(2,1)} custom-call(s32[1]{0:T(128)} %bitcast.6.core_ref, f32[120,8,128]{2,1,0:T(8,128)S(1)} %shard_map.140.mine_ref, bf16[16,64,128]{2,1,0:T(8,128)(2,1)S(1)} %collective-permute-done.other_ref), custom_call_target="tpu_custom_call" | custom-call | tf_op jit(solution)/shard_map/pallas_call | solution.py:373
  (39 shorter events, 0.5 us)
Async XLA Ops:
  0.0 25.5 %copy-start = (s32[10]{0:T(128)S(1)}, s32[10]{0:T(128)}, u32[]{:S(2)}) copy-start(s32[10]{0:T(128)} %param.23) | copy-start | bytes 124
  5.8 11.6 %copy-start.3 = (bf16[40,8,2,128]{3,2,1,0:T(2,128)(2,1)S(1)}, bf16[40,8,2,128]{3,2,1,0:T(2,128)(2,1)}, u32[]{:S(2)}) copy-start(bf16[40,8,2,128]{3,2,1,0:T(2,128)(2,1)} %param.19) | copy-start | bytes 491524
  5.8 11.7 %copy-start.4 = (bf16[3,40,2,128]{3,2,1,0:T(2,128)(2,1)S(1)}, bf16[3,40,2,128]{3,2,1,0:T(2,128)(2,1)}, u32[]{:S(2)}) copy-start(bf16[3,40,2,128]{3,2,1,0:T(2,128)(2,1)} %param.21) | copy-start | bytes 184324
  5.9 14.0 %copy-start.5 = (s32[160]{0:T(256)S(1)}, s32[160]{0:T(256)}, u32[]{:S(2)}) copy-start(s32[160]{0:T(256)} %slot_ref.1) | copy-start | bytes 1924
  5.9 15.4 %copy-start.6 = (s32[3,10]{1,0:T(4,128)S(1)}, s32[3,10]{1,0:T(4,128)}, u32[]{:S(2)}) copy-start(s32[3,10]{1,0:T(4,128)} %param.24) | copy-start | bytes 364
  5.9 36.4 %all-to-all-start.1 = ((bf16[8,1008,128]{2,1,0:T(8,128)(2,1)}), bf16[8,1008,128]{2,1,0:T(8,128)(2,1)S(1)}, u32[]{:S(2)}, u32[]{:S(2)}) async-start(bf16[8,1008,128]{2,1,0:T(8,128)(2,1)} %get-tuple-element.21), calls=%async_computation.1 | async-start | bytes 4128768 | tf_op jit(solution)/shard_map/all_to_all | solution.py:259
  16.4 25.9 %copy-start.1 = (bf16[192,192]{1,0:T(8,128)(2,1)S(1)}, bf16[192,192]{1,0:T(8,128)(2,1)}, u32[]{:S(2)}) copy-start(bf16[192,192]{1,0:T(8,128)(2,1)} %constant.248.clone.order_ref) | copy-start | bytes 221188
  16.4 25.9 %copy-start.2 = (f32[8,192]{1,0:T(8,128)S(1)}, f32[8,192]{1,0:T(8,128)}, u32[]{:S(2)}) copy-start(f32[8,192]{1,0:T(8,128)} %constant.249.clone.heads_ref) | copy-start | bytes 18436
  102.5 9.9 %collective-permute-start = (bf16[16,64,128]{2,1,0:T(8,128)(2,1)S(1)}, bf16[16,64,128]{2,1,0:T(8,128)(2,1)S(1)}, u32[]{:S(2)}, u32[]{:S(2)}) collective-permute-start(bf16[16,64,128]{2,1,0:T(8,128)(2,1)S(1)} %all_to_all.27.mine_ref), channel_id=1, source_target_pairs={{0,16},{16,0},{32,48},{48,32},{64,80},{80,64},{96,112},{112,96},{1... | collective-permute-start | bytes 786440 | tf_op jit(solution)/shard_map/ppermute | solution.py:364
